TPU v7x, 256 devices: a whole 4x4x8 slice. The times are simulated.
256 devices in a mesh: sec: 8 (over x, y_lo), ctx: 32 (over z, y_hi, core).
Axes of the slice: x: 4, y: 4 (y_hi: 2, y_lo: 2; y = y_hi * 2 + y_lo), z: 8, core: 2. Of those that a mesh axis runs over, the one named last changes fastest.
Arguments:
- hidden_state: bfloat16 [8, 4096, 4096], P('sec', 'ctx'), may hold values from -8 to 8
- queries: bfloat16 [8, 4096, 4096], P('sec', 'ctx'), may hold values from -6 to 6
- key_vectors: bfloat16 [8, 4096, 4096], P('sec', 'ctx'), may hold values from -4.5 to 4.5
- value_vectors: bfloat16 [8, 4096, 4096], P('sec', 'ctx'), may hold values from -6 to 6
- modulation: float32 [32, 3, 4096], replicated, may hold values from -3 to 3
- down_weight: bfloat16 [4096, 256], replicated, may hold values from -0.09375 to 0.09375
- conv_weight: bfloat16 [3, 3, 3, 256, 256], replicated, may hold values from -0.078125 to 0.078125
- clip_frames: int32 [8], replicated, may hold values from 16 to 64, as said below
- destination: int32 [8], replicated, may hold values from 0 to 7, as said below
- timestep: int32 [8], replicated, may hold values from 0 to 31
Outputs:
- upsampled: bfloat16 [8, 4096, 256], P('sec', 'ctx')
Inputs may be any that keep to these rules, and one draw needn't show every extreme that they name: `clip_frames`: one section's clip fills all 64 frames. `destination`: every upsampler group receives exactly one clip; some group d receives the clip of section (d + 4) mod 8.
All inputs are finite; a program needn't handle non-finite values.
Results may differ from a plain program's by a relative error of at most 0.0063.
Values may be sent and summed in bfloat16 or wider, within the bound.
A program may use at most 64 MiB of HBM per device.

v0:
```python
import math
import jax
import jax.numpy as jnp
from jax import lax
from jax.sharding import PartitionSpec as P

HEADS = 32
HH = 8
WW = 8


def extended(block, sides, width):
    for axis, dim in sides:
        count = lax.axis_size(axis)
        forward = [(i, i + 1) for i in range(count - 1)]
        backward = [(target, source) for source, target in forward]
        low = lax.ppermute(
            lax.slice_in_dim(block, block.shape[dim] - width, None, axis=dim), axis, forward
        )
        high = lax.ppermute(lax.slice_in_dim(block, 0, width, axis=dim), axis, backward)
        block = jnp.concatenate([low, block, high], axis=dim)
    return block


def attend_heads(tensors, frames):
    query_part, key_part, value_part = tensors
    item_count, seq_len, local_heads, head_size = query_part.shape
    block_rows = min(512, seq_len)
    score_scale = 1.0 / math.sqrt(head_size)
    positions = jnp.arange(seq_len, dtype=jnp.int32) // (HH * WW)
    key_valid = positions < frames
    query_blocks = query_part.reshape(
        item_count, seq_len // block_rows, block_rows, local_heads, head_size
    )
    query_blocks = jnp.moveaxis(query_blocks, 1, 0)

    def one_block(query_block):
        scores = (
            jnp.einsum("nqhd,nkhd->nhqk", query_block, key_part, preferred_element_type=jnp.float32)
            * score_scale
        )
        scores = jnp.where(key_valid[None, None, None, :], scores, -jnp.inf)
        weights = jnp.exp(scores - jnp.max(scores, axis=3, keepdims=True))
        row_total = jnp.sum(weights, axis=3)
        rounded = weights.astype(jnp.bfloat16)
        product = jnp.einsum(
            "nhqk,nkhd->nqhd", rounded, value_part, preferred_element_type=jnp.float32
        )
        return (product / jnp.moveaxis(row_total, 1, 2)[..., None]).astype(jnp.bfloat16)

    result = lax.map(one_block, query_blocks)
    return jnp.moveaxis(result, 0, 1).reshape(item_count, seq_len, local_heads, head_size)


def adapt_input(block_out, mod_rows, down_weight):
    wide_values = block_out.astype(jnp.float32)
    centre = jnp.mean(wide_values, axis=-1, keepdims=True)
    spread = jnp.mean(jnp.square(wide_values - centre), axis=-1, keepdims=True)
    normed = (
        (wide_values - centre) * lax.rsqrt(spread + 1e-06) * (1.0 + mod_rows[1]) + mod_rows[0]
    ).astype(jnp.bfloat16)
    return jnp.einsum(
        "std,dc->stc", normed, down_weight, preferred_element_type=jnp.float32
    ).astype(jnp.bfloat16)


def body(
    hidden_state,
    queries,
    key_vectors,
    value_vectors,
    modulation,
    down_weight,
    conv_weight,
    clip_frames,
    destination,
    timestep,
):
    my_section = lax.axis_index("sec")
    my_place = lax.axis_index("ctx")
    sections, tok_rows, model_width = hidden_state.shape
    head_size = model_width // HEADS
    own_frames = clip_frames[my_section]
    my_step = timestep[my_section]

    def by_heads(tensor):
        return tensor.reshape(sections, tok_rows, HEADS, head_size)

    local_out = attend_heads(
        (
            lax.all_to_all(by_heads(queries), "ctx", split_axis=2, concat_axis=1, tiled=True),
            lax.all_to_all(by_heads(key_vectors), "ctx", split_axis=2, concat_axis=1, tiled=True),
            lax.all_to_all(by_heads(value_vectors), "ctx", split_axis=2, concat_axis=1, tiled=True),
        ),
        own_frames,
    )
    attended = lax.all_to_all(local_out, "ctx", split_axis=1, concat_axis=2, tiled=True)
    attended = attended.reshape(sections, tok_rows, model_width)
    block_out = (
        hidden_state.astype(jnp.float32) + modulation[my_step, 2] * attended.astype(jnp.float32)
    ).astype(jnp.bfloat16)
    section_ids = jnp.arange(destination.shape[0], dtype=jnp.int32)
    source = jnp.sum(jnp.where(destination == my_section, section_ids, 0))
    own_projected = adapt_input(block_out, modulation[my_step], down_weight)
    gathered = lax.all_gather(own_projected, "sec", axis=0, tiled=True)
    first_row = jnp.int32(0)
    piece_rows = gathered.shape[0]
    offset = jnp.clip(source, 0, piece_rows - 1)
    chosen = lax.dynamic_index_in_dim(gathered, offset, 0, keepdims=True)
    inside = (source >= first_row) & (source < first_row + piece_rows)
    projected = jnp.where(inside, chosen, jnp.zeros_like(own_projected))
    frames_here = tok_rows // (HH * WW)
    frame_number = my_place * frames_here + jnp.arange(frames_here, dtype=jnp.int32)
    keep_frame = (frame_number < clip_frames[source])[None, :, None, None, None]
    clip_cells = jnp.where(keep_frame, projected.reshape(sections, frames_here, HH, WW, -1), 0)
    padded = extended(clip_cells, (("ctx", 1),), 1)
    convolved = lax.conv_general_dilated(
        padded,
        conv_weight,
        (1, 1, 1),
        ((0, 0), (1, 1), (1, 1)),
        dimension_numbers=("NDHWC", "DHWIO", "NDHWC"),
        preferred_element_type=jnp.float32,
    )
    upsampled = jnp.where(keep_frame, clip_cells.astype(jnp.float32) + convolved, 0.0).astype(
        jnp.bfloat16
    )
    return upsampled.reshape(sections, tok_rows, -1)


def solution(mesh):
    in_specs = (
        P("sec", "ctx", None),
        P("sec", "ctx", None),
        P("sec", "ctx", None),
        P("sec", "ctx", None),
        P(),
        P(),
        P(),
        P(),
        P(),
        P(),
    )
    out_specs = P("sec", "ctx", None)
    return jax.shard_map(body, mesh=mesh, in_specs=in_specs, out_specs=out_specs, check_vma=False)
```

profile of v0, /device:TPU:1, one launch (start us, length us, event | category | flops | bytes accessed | tf_op | source)
XLA Modules:
  0.0 303.9 jit_solution(16420890058449033828)
XLA Ops:
  0.0 2.4 copy.39
  2.4 12.8 %all-to-all-start = ((bf16[1,128,32,128]{1,3,0,2:T(8,128)(2,1)}), bf16[1,128,32,128]{1,3,0,2:T(8,128)(2,1)}, u32[]{:S(2)}, u32[]{:S(2)}) async-start(bf16[1,128,32,128]{1,3,0,2:T(8,128)(2,1)} %bitcast.99), calls=%async_computation | async-start | bytes 2097152 | tf_op jit(solution)/shard_map/all_to_all | solution.py:91
  17.5 25.9 %all-to-all-done = bf16[1,128,32,128]{1,3,0,2:T(8,128)(2,1)} async-done(((bf16[1,128,32,128]{1,3,0,2:T(8,128)(2,1)}), bf16[1,128,32,128]{1,3,0,2:T(8,128)(2,1)}, u32[]{:S(2)}, u32[]{:S(2)}) %all-to-all-start) | async-done | bytes 1048608 | tf_op jit(solution)/shard_map/all_to_all | solution.py:91
  43.4 5.8 %all-to-all-start.1 = ((bf16[1,128,32,128]{1,3,0,2:T(8,128)(2,1)}), bf16[1,128,32,128]{1,3,0,2:T(8,128)(2,1)}, u32[]{:S(2)}, u32[]{:S(2)}) async-start(bf16[1,128,32,128]{1,3,0,2:T(8,128)(2,1)} %bitcast.98), calls=%async_computation.1 | async-start | bytes 2097152 | tf_op jit(solution)/shard_map/all_to_all | solution.py:92
  51.6 25.9 %all-to-all-done.1 = bf16[1,128,32,128]{1,3,0,2:T(8,128)(2,1)} async-done(((bf16[1,128,32,128]{1,3,0,2:T(8,128)(2,1)}), bf16[1,128,32,128]{1,3,0,2:T(8,128)(2,1)}, u32[]{:S(2)}, u32[]{:S(2)}) %all-to-all-start.1) | async-done | bytes 1048608 | tf_op jit(solution)/shard_map/all_to_all | solution.py:92
  77.5 5.9 %all-to-all-start.2 = ((bf16[1,128,32,128]{1,3,0,2:T(8,128)(2,1)}), bf16[1,128,32,128]{1,3,0,2:T(8,128)(2,1)}, u32[]{:S(2)}, u32[]{:S(2)}) async-start(bf16[1,128,32,128]{1,3,0,2:T(8,128)(2,1)} %bitcast.97), calls=%async_computation.2 | async-start | bytes 2097152 | tf_op jit(solution)/shard_map/all_to_all | solution.py:93
  91.1 20.4 %all-to-all-done.2 = bf16[1,128,32,128]{1,3,0,2:T(8,128)(2,1)} async-done(((bf16[1,128,32,128]{1,3,0,2:T(8,128)(2,1)}), bf16[1,128,32,128]{1,3,0,2:T(8,128)(2,1)}, u32[]{:S(2)}, u32[]{:S(2)}) %all-to-all-start.2) | async-done | bytes 1048608 | tf_op jit(solution)/shard_map/all_to_all | solution.py:93
  113.8 63.7 %while.11 = (s32[]{:T(128)}, bf16[8,1,512,1,128]{4,2,3,1,0:T(8,128)(2,1)}, bf16[8,1,512,1,128]{4,2,3,1,0:T(8,128)(2,1)}, bf16[1,4096,1,128]{3,1,2,0:T(8,128)(2,1...) while((s32[]{:T(128)}, bf16[8,1,512,1,128]{4,2,3,1,0:T(8,128)(2,1)}, ...), condition=%wide.region_4.5_spmd.clone, body=%wide.region_1.4_spmd.clone.sunk | while | flops 1096977408 | bytes 31746172 | solution.py:51
  114.4 2.7 fusion.69
  119.3 2.4 fusion.71
  122.4 2.7 fusion.69
  127.3 2.4 fusion.71
  130.4 2.7 fusion.69
  138.3 2.7 fusion.69
  146.3 2.7 fusion.69
  151.2 2.4 fusion.71
  154.2 2.7 fusion.69
  162.2 2.7 fusion.69
  167.1 2.4 fusion.71
  170.2 2.7 fusion.69
  177.5 4.3 %copy.55 = bf16[1,4096,1,128]{3,2,0,1:T(2,128)(2,1)} copy(bf16[1,4096,1,128]{3,1,2,0:T(8,128)(2,1)} %bitcast.101) | data formatting | bytes 2097152 | tf_op jit(solution)/shard_map/reshape;transpose | solution.py:52
  182.3 24.3 %reduce.6 = bf16[4096,128]{1,0:T(8,128)(2,1)} reduce(bf16[4096,1,1,128]{3,2,1,0:T(2,128)(2,1)} %bitcast.95, bf16[]{:T(256)} %broadcast.118), dimensions={1,2}, to_apply=%bitcast.83.reduce_sub_computation | reduce | bytes 2097154
  208.8 5.9 %all-to-all-start.3 = ((bf16[32,2,8192]{2,1,0:T(2,128)(2,1)}), bf16[32,2,8192]{2,1,0:T(2,128)(2,1)}, u32[]{:S(2)}, u32[]{:S(2)}) async-start(bf16[32,2,8192]{2,1,0:T(2,128)(2,1)} %reshape.170), calls=%async_computation.3 | async-start | bytes 2097152 | tf_op jit(solution)/shard_map/all_to_all | solution.py:97
  221.9 20.8 %all-to-all-done.3 = bf16[32,2,8192]{2,1,0:T(2,128)(2,1)} async-done(((bf16[32,2,8192]{2,1,0:T(2,128)(2,1)}), bf16[32,2,8192]{2,1,0:T(2,128)(2,1)}, u32[]{:S(2)}, u32[]{:S(2)}) %all-to-all-start.3) | async-done | bytes 1048608 | tf_op jit(solution)/shard_map/all_to_all | solution.py:97
  242.7 5.8 %reshape.171 = bf16[4096,1,1,128]{3,2,1,0:T(2,128)(2,1)} reshape(bf16[32,2,8192]{2,1,0:T(2,128)(2,1)} %all-to-all-done.3) | data formatting | bytes 2097152
  248.4 3.8 %bitcast_convert_fusion = f32[1,4096,1,128]{3,2,0,1:T(1,128)S(1)} fusion(bf16[4096,1,1,128]{3,2,1,0:T(2,128)(2,1)} %reshape.171), kind=kLoop, calls=%fused_computation.65 | loop fusion | flops 524288 | bytes 3145728 | tf_op jit(solution)/shard_map/convert_element_type | solution.py:100
  252.2 2.6 copy.50
  254.8 2.7 reshape.164
  261.0 23.3 %all-gather = bf16[1024,256]{1,0:T(8,128)(2,1)S(1)} all-gather(bf16[128,256]{1,0:T(8,128)(2,1)S(1)} %convolution_convert_fusion), channel_id=2, replica_groups=mesh['sec'=8,'ctx'=32] {'sec'}, dimensions={0}, use_global_device_ids=true | all-gather | bytes 589824 | tf_op jit(solution)/shard_map/all_gather | solution.py:105
  284.6 9.2 %collective-permute-start.1 = (bf16[1,1,8,8,256]{4,0,3,2,1:T(2,128)(2,1)S(1)}, bf16[1,1,8,8,256]{4,0,3,2,1:T(2,128)(2,1)S(1)}, u32[]{:S(2)}, u32[]{:S(2)}) collective-permute-start(bf16[1,1,8,8,256]{4,0,3,2,1:T(2,128)(2,1)S(1)} %get-tuple-element.97), channel_id=1, source_target_pairs={{1,0},{2,1},{3,2},{4,3},{5,4},{6,5},{7,6},{8,7},{9,8},{10,9},{11,1... | collective-permute-start | bytes 98312 | tf_op jit(solution)/shard_map/ppermute | solution.py:20
  293.8 4.8 %collective-permute-start = (bf16[1,1,8,8,256]{4,0,3,2,1:T(2,128)(2,1)S(1)}, bf16[1,1,8,8,256]{4,0,3,2,1:T(2,128)(2,1)S(1)}, u32[]{:S(2)}, u32[]{:S(2)}) collective-permute-start(bf16[1,1,8,8,256]{4,0,3,2,1:T(2,128)(2,1)S(1)} %get-tuple-element.96), channel_id=1, source_target_pairs={{0,1},{1,2},{2,3},{3,4},{4,5},{5,6},{6,7},{7,8},{8,9},{9,10},{10,1... | collective-permute-start | bytes 98312 | tf_op jit(solution)/shard_map/ppermute | solution.py:17
  300.0 3.2 %fusion.42 = bf16[1,2,8,8,256]{4,0,3,2,1:T(2,128)(2,1)S(1)} fusion(bf16[3,3,3,256,256]{4,3,2,1,0:T(8,128)(2,1)S(1)} %copy-done, bf16[1,1,8,8,256]{4,0,3,2,1:T(2,128)(2,1)S(1)} %collective-permute-done.1, bf16[1,2,8,8,256]{4,0,3,2,1:T(2,128)(2,1)S(1)} %broadcast_select_fusion, bf16[1,1,8,8,256]{4,0,3,2,1:T(2,128)(2,1)S(1)} %collective-permute-done, ...), kind=kOutput, calls=%fused_computation.40 | convolution fusion | flops 381157376 | bytes 3735554 | tf_op jit(solution)/shard_map/conv_general_dilated | solution.py:117
  (76 shorter events, 56.2 us)
Async XLA Ops:
  0.0 300.0 %copy-start = (bf16[3,3,3,256,256]{4,3,2,1,0:T(8,128)(2,1)S(1)}, bf16[3,3,3,256,256]{4,3,2,1,0:T(8,128)(2,1)}, u32[]{:S(2)}) copy-start(bf16[3,3,3,256,256]{4,3,2,1,0:T(8,128)(2,1)} %param.18) | copy-start | bytes 10616836
  2.4 41.0 %all-to-all-start = ((bf16[1,128,32,128]{1,3,0,2:T(8,128)(2,1)}), bf16[1,128,32,128]{1,3,0,2:T(8,128)(2,1)}, u32[]{:S(2)}, u32[]{:S(2)}) async-start(bf16[1,128,32,128]{1,3,0,2:T(8,128)(2,1)} %bitcast.99), calls=%async_computation | async-start | bytes 2097152 | tf_op jit(solution)/shard_map/all_to_all | solution.py:91
  43.4 34.0 %all-to-all-start.1 = ((bf16[1,128,32,128]{1,3,0,2:T(8,128)(2,1)}), bf16[1,128,32,128]{1,3,0,2:T(8,128)(2,1)}, u32[]{:S(2)}, u32[]{:S(2)}) async-start(bf16[1,128,32,128]{1,3,0,2:T(8,128)(2,1)} %bitcast.98), calls=%async_computation.1 | async-start | bytes 2097152 | tf_op jit(solution)/shard_map/all_to_all | solution.py:92
  49.3 34.0 %copy-start.7 = (s32[8]{0:T(128)S(1)}, s32[8]{0:T(128)}, u32[]{:S(2)}) copy-start(s32[8]{0:T(128)} %param.20) | copy-start | bytes 100
  49.3 36.6 %copy-start.4 = (s32[8]{0:T(128)S(1)}, s32[8]{0:T(128)}, u32[]{:S(2)}) copy-start(s32[8]{0:T(128)} %param.19) | copy-start | bytes 100
  77.5 34.0 %all-to-all-start.2 = ((bf16[1,128,32,128]{1,3,0,2:T(8,128)(2,1)}), bf16[1,128,32,128]{1,3,0,2:T(8,128)(2,1)}, u32[]{:S(2)}, u32[]{:S(2)}) async-start(bf16[1,128,32,128]{1,3,0,2:T(8,128)(2,1)} %bitcast.97), calls=%async_computation.2 | async-start | bytes 2097152 | tf_op jit(solution)/shard_map/all_to_all | solution.py:93
  117.2 2.2 copy-start.1
  125.1 2.2 copy-start.1
  133.1 2.2 copy-start.1
  141.1 2.2 copy-start.1
  149.0 2.2 copy-start.1
  157.0 2.2 copy-start.1
  164.9 2.2 copy-start.1
  172.9 2.2 copy-start.1
  206.7 10.0 %copy-start.8 = (s32[8]{0:T(128)S(1)}, s32[8]{0:T(128)}, u32[]{:S(2)}) copy-start(s32[8]{0:T(128)} %param.21) | copy-start | bytes 100
  208.8 33.9 %all-to-all-start.3 = ((bf16[32,2,8192]{2,1,0:T(2,128)(2,1)}), bf16[32,2,8192]{2,1,0:T(2,128)(2,1)}, u32[]{:S(2)}, u32[]{:S(2)}) async-start(bf16[32,2,8192]{2,1,0:T(2,128)(2,1)} %reshape.170), calls=%async_computation.3 | async-start | bytes 2097152 | tf_op jit(solution)/shard_map/all_to_all | solution.py:97
  257.5 2.9 copy-start.2
  257.5 2.9 copy-start.3
  257.5 2.9 copy-start.6
  260.4 23.9 %copy-start.5 = (pred[2]{0:T(512)(128)(4,1)S(1)}, pred[2]{0:T(512)(128)(4,1)}, u32[]{:S(2)}) copy-start(pred[2]{0:T(512)(128)(4,1)} %add_compare_fusion) | copy-start | bytes 10
  284.6 14.0 %collective-permute-start.1 = (bf16[1,1,8,8,256]{4,0,3,2,1:T(2,128)(2,1)S(1)}, bf16[1,1,8,8,256]{4,0,3,2,1:T(2,128)(2,1)S(1)}, u32[]{:S(2)}, u32[]{:S(2)}) collective-permute-start(bf16[1,1,8,8,256]{4,0,3,2,1:T(2,128)(2,1)S(1)} %get-tuple-element.97), channel_id=1, source_target_pairs={{1,0},{2,1},{3,2},{4,3},{5,4},{6,5},{7,6},{8,7},{9,8},{10,9},{11,1... | collective-permute-start | bytes 98312 | tf_op jit(solution)/shard_map/ppermute | solution.py:20
  293.8 6.2 %collective-permute-start = (bf16[1,1,8,8,256]{4,0,3,2,1:T(2,128)(2,1)S(1)}, bf16[1,1,8,8,256]{4,0,3,2,1:T(2,128)(2,1)S(1)}, u32[]{:S(2)}, u32[]{:S(2)}) collective-permute-start(bf16[1,1,8,8,256]{4,0,3,2,1:T(2,128)(2,1)S(1)} %get-tuple-element.96), channel_id=1, source_target_pairs={{0,1},{1,2},{2,3},{3,4},{4,5},{5,6},{6,7},{7,8},{8,9},{9,10},{10,1... | collective-permute-start | bytes 98312 | tf_op jit(solution)/shard_map/ppermute | solution.py:17
where the time goes:
time: 305 us; the launch traced here: 304 us
  waiting for transfers between devices  94.3 us (31%)
  other arithmetic  56.8 us (19%)
  matrix products  45.1 us (15%)
  starting transfers between devices  44.4 us (15%)
  local copies, waits for them, and re-layouts  33.8 us (11%)
  blocking collectives  23.3 us (8%)
  between operations  6.06 us (2%)
    all_to_all x1, waiting for transfers between devices, body(): lax.all_to_all(by_heads(queries), 'ctx', split_axis=2, concat_axis=1, til...  25.9 us
    all_to_all x1, waiting for transfers between devices, body(): lax.all_to_all(by_heads(key_vectors), 'ctx', split_axis=2, concat_axis=1,...  25.9 us
    unnamed x1, other arithmetic  24.3 us
    all_gather x1, blocking collectives, body(): gathered = lax.all_gather(own_projected, 'sec', axis=0, tiled=True)  23.3 us
    dot_general x8, matrix products, one_block(): jnp.einsum('nqhd,nkhd->nhqk', query_block, key_part, preferred_element_ty...  22 us
    all_to_all x1, waiting for transfers between devices, body(): lax.all_to_all(local_out, 'ctx', split_axis=1, concat_axis=2, tiled=True)  20.8 us
    all_to_all x1, waiting for transfers between devices, body(): lax.all_to_all(by_heads(value_vectors), 'ctx', split_axis=2, concat_axis=...  20.4 us
    dot_general x8, matrix products, one_block(): jnp.einsum('nhqk,nkhd->nqhd', rounded, value_part, preferred_element_type...  19.3 us
  transfers between devices with their start and end apart: 6, of which 5 were waited for; matrix products, arithmetic and copies ran while one was open for 4% of the time, Pallas kernels for 0%

commit v1 on v0

--- a/solution.py
+++ b/solution.py
@@ -102,7 +102,15 @@
     section_ids = jnp.arange(destination.shape[0], dtype=jnp.int32)
     source = jnp.sum(jnp.where(destination == my_section, section_ids, 0))
     own_projected = adapt_input(block_out, modulation[my_step], down_weight)
-    gathered = lax.all_gather(own_projected, "sec", axis=0, tiled=True)
+    gathered = jnp.concatenate(
+        lax.all_to_all(
+            jnp.stack([own_projected] * lax.axis_size("sec"), 0),
+            axis_name="sec",
+            split_axis=0,
+            concat_axis=0,
+        ),
+        0,
+    )
     first_row = jnp.int32(0)
     piece_rows = gathered.shape[0]
     offset = jnp.clip(source, 0, piece_rows - 1)

time: 305 us -> 293 us (0.961)
  blocking collectives: 23.3 us -> 0 us
  waiting for transfers between devices: 94.3 us -> 103 us
    all_gather x1 -> x0, blocking collectives: 23.3 us -> none  [body(): gathered = lax.all_gather(own_projected, 'sec', axis=0, tiled=True)]
    all_to_all x0 -> x1, waiting for transfers between devices: none -> 5.43 us  [body(): lax.all_to_all(jnp.stack([own_projected] * lax.axis_size('sec'), 0), axis...]
    ppermute x1, starting transfers between devices: 9.18 us -> 4.47 us  [extended(): lax.ppermute(lax.slice_in_dim(block, 0, width, axis=dim), axis, backward)]
    all_to_all x0 -> x1, starting transfers between devices: none -> 4.15 us  [body(): lax.all_to_all(jnp.stack([own_projected] * lax.axis_size('sec'), 0), axis...]
    unnamed x23 -> x21, local copies, waits for them, and re-layouts: 16 us -> 16.1 us
  transfers between devices with their start and end apart: 6 -> 7, of which waited for: 5 -> 6; matrix products, arithmetic and copies ran while one was open for 4% -> 5% of each run, Pallas kernels for 0% -> 0%
where the time goes in v1:
time: 293 us; the launch traced here: 291 us
  waiting for transfers between devices  103 us (35%)
  other arithmetic  57.5 us (20%)
  matrix products  45.2 us (15%)
  starting transfers between devices  44.6 us (15%)
  local copies, waits for them, and re-layouts  34.7 us (12%)
  between operations  5.88 us (2%)
    all_to_all x1, waiting for transfers between devices, body(): lax.all_to_all(by_heads(queries), 'ctx', split_axis=2, concat_axis=1, til...  25.9 us
    all_to_all x1, waiting for transfers between devices, body(): lax.all_to_all(by_heads(key_vectors), 'ctx', split_axis=2, concat_axis=1,...  25.9 us
    unnamed x1, other arithmetic  24.4 us
    all_to_all x1, waiting for transfers between devices, body(): lax.all_to_all(local_out, 'ctx', split_axis=1, concat_axis=2, tiled=True)  23.8 us
    dot_general x8, matrix products, one_block(): jnp.einsum('nqhd,nkhd->nhqk', query_block, key_part, preferred_element_ty...  22 us
    all_to_all x1, waiting for transfers between devices, body(): lax.all_to_all(by_heads(value_vectors), 'ctx', split_axis=2, concat_axis=...  20.5 us
    dot_general x8, matrix products, one_block(): jnp.einsum('nhqk,nkhd->nqhd', rounded, value_part, preferred_element_type...  19.4 us
    reduce_sum x8, other arithmetic, one_block(): row_total = jnp.sum(weights, axis=3)  17.3 us
  transfers between devices with their start and end apart: 7, of which 6 were waited for; matrix products, arithmetic and copies ran while one was open for 5% of the time, Pallas kernels for 0%

profile of v1, /device:TPU:1, one launch (start us, length us, event | category | flops | bytes accessed | tf_op | source)
XLA Modules:
  0.0 290.8 jit_solution(4026313118678740126)
XLA Ops:
  2.4 12.8 %all-to-all-start = ((bf16[1,128,32,128]{1,3,0,2:T(8,128)(2,1)}), bf16[1,128,32,128]{1,3,0,2:T(8,128)(2,1)}, u32[]{:S(2)}, u32[]{:S(2)}) async-start(bf16[1,128,32,128]{1,3,0,2:T(8,128)(2,1)} %bitcast.98), calls=%async_computation | async-start | bytes 2097152 | tf_op jit(solution)/shard_map/all_to_all | solution.py:91
  17.5 25.9 %all-to-all-done = bf16[1,128,32,128]{1,3,0,2:T(8,128)(2,1)} async-done(((bf16[1,128,32,128]{1,3,0,2:T(8,128)(2,1)}), bf16[1,128,32,128]{1,3,0,2:T(8,128)(2,1)}, u32[]{:S(2)}, u32[]{:S(2)}) %all-to-all-start) | async-done | bytes 1048608 | tf_op jit(solution)/shard_map/all_to_all | solution.py:91
  43.4 5.8 %all-to-all-start.1 = ((bf16[1,128,32,128]{1,3,0,2:T(8,128)(2,1)}), bf16[1,128,32,128]{1,3,0,2:T(8,128)(2,1)}, u32[]{:S(2)}, u32[]{:S(2)}) async-start(bf16[1,128,32,128]{1,3,0,2:T(8,128)(2,1)} %bitcast.97), calls=%async_computation.1 | async-start | bytes 2097152 | tf_op jit(solution)/shard_map/all_to_all | solution.py:92
  51.6 25.9 %all-to-all-done.1 = bf16[1,128,32,128]{1,3,0,2:T(8,128)(2,1)} async-done(((bf16[1,128,32,128]{1,3,0,2:T(8,128)(2,1)}), bf16[1,128,32,128]{1,3,0,2:T(8,128)(2,1)}, u32[]{:S(2)}, u32[]{:S(2)}) %all-to-all-start.1) | async-done | bytes 1048608 | tf_op jit(solution)/shard_map/all_to_all | solution.py:92
  77.5 5.9 %all-to-all-start.2 = ((bf16[1,128,32,128]{1,3,0,2:T(8,128)(2,1)}), bf16[1,128,32,128]{1,3,0,2:T(8,128)(2,1)}, u32[]{:S(2)}, u32[]{:S(2)}) async-start(bf16[1,128,32,128]{1,3,0,2:T(8,128)(2,1)} %bitcast.96), calls=%async_computation.2 | async-start | bytes 2097152 | tf_op jit(solution)/shard_map/all_to_all | solution.py:93
  91.0 20.5 %all-to-all-done.2 = bf16[1,128,32,128]{1,3,0,2:T(8,128)(2,1)} async-done(((bf16[1,128,32,128]{1,3,0,2:T(8,128)(2,1)}), bf16[1,128,32,128]{1,3,0,2:T(8,128)(2,1)}, u32[]{:S(2)}, u32[]{:S(2)}) %all-to-all-start.2) | async-done | bytes 1048608 | tf_op jit(solution)/shard_map/all_to_all | solution.py:93
  113.8 64.0 %while.11 = (s32[]{:T(128)}, bf16[8,1,512,1,128]{4,2,3,1,0:T(8,128)(2,1)}, bf16[8,1,512,1,128]{4,2,3,1,0:T(8,128)(2,1)}, bf16[1,4096,1,128]{3,1,2,0:T(8,128)(2,1...) while((s32[]{:T(128)}, bf16[8,1,512,1,128]{4,2,3,1,0:T(8,128)(2,1)}, ...), condition=%wide.region_4.5_spmd.clone, body=%wide.region_1.4_spmd.clone.sunk | while | flops 1096977408 | bytes 31746172 | solution.py:51
  114.4 2.7 fusion.69
  122.4 2.7 fusion.69
  127.3 2.4 fusion.71
  130.4 2.7 fusion.69
  135.4 2.4 fusion.71
  138.4 2.7 fusion.69
  143.4 2.4 fusion.71
  146.4 2.7 fusion.69
  154.4 2.7 fusion.69
  162.4 2.7 fusion.69
  167.3 2.4 fusion.71
  170.4 2.7 fusion.69
  177.8 4.3 %copy.55 = bf16[1,4096,1,128]{3,2,0,1:T(2,128)(2,1)} copy(bf16[1,4096,1,128]{3,1,2,0:T(8,128)(2,1)} %bitcast.100) | data formatting | bytes 2097152 | tf_op jit(solution)/shard_map/reshape;transpose | solution.py:52
  182.6 24.4 %reduce.6 = bf16[4096,128]{1,0:T(8,128)(2,1)} reduce(bf16[4096,1,1,128]{3,2,1,0:T(2,128)(2,1)} %bitcast.94, bf16[]{:T(256)} %broadcast.152), dimensions={1,2}, to_apply=%bitcast.82.reduce_sub_computation | reduce | bytes 2097154
  209.2 5.9 %all-to-all-start.3 = ((bf16[32,2,8192]{2,1,0:T(2,128)(2,1)}), bf16[32,2,8192]{2,1,0:T(2,128)(2,1)}, u32[]{:S(2)}, u32[]{:S(2)}) async-start(bf16[32,2,8192]{2,1,0:T(2,128)(2,1)} %reshape.181), calls=%async_computation.3 | async-start | bytes 2097152 | tf_op jit(solution)/shard_map/all_to_all | solution.py:97
  219.3 23.8 %all-to-all-done.3 = bf16[32,2,8192]{2,1,0:T(2,128)(2,1)} async-done(((bf16[32,2,8192]{2,1,0:T(2,128)(2,1)}), bf16[32,2,8192]{2,1,0:T(2,128)(2,1)}, u32[]{:S(2)}, u32[]{:S(2)}) %all-to-all-start.3) | async-done | bytes 1048608 | tf_op jit(solution)/shard_map/all_to_all | solution.py:97
  243.1 5.8 %reshape.182 = bf16[4096,1,1,128]{3,2,1,0:T(2,128)(2,1)} reshape(bf16[32,2,8192]{2,1,0:T(2,128)(2,1)} %all-to-all-done.3) | data formatting | bytes 2097152
  248.8 3.8 %bitcast_convert_fusion = f32[1,4096,1,128]{3,2,0,1:T(1,128)S(1)} fusion(bf16[4096,1,1,128]{3,2,1,0:T(2,128)(2,1)} %reshape.182), kind=kLoop, calls=%fused_computation.65 | loop fusion | flops 524288 | bytes 3145728 | tf_op jit(solution)/shard_map/convert_element_type | solution.py:100
  252.6 2.6 copy.50
  255.2 2.7 reshape.176
  262.2 4.2 %all-to-all-start.4 = ((bf16[8,1,128,256]{3,2,1,0:T(8,128)(2,1)}), bf16[8,1,128,256]{3,2,1,0:T(8,128)(2,1)}, u32[]{:S(2)}, u32[]{:S(2)}) async-start(bf16[8,1,128,256]{3,2,1,0:T(8,128)(2,1)} %stack.2), calls=%async_computation.4 | async-start | bytes 1048576 | tf_op jit(solution)/shard_map/all_to_all | solution.py:106
  268.9 5.4 %all-to-all-done.4 = bf16[8,1,128,256]{3,2,1,0:T(8,128)(2,1)} async-done(((bf16[8,1,128,256]{3,2,1,0:T(8,128)(2,1)}), bf16[8,1,128,256]{3,2,1,0:T(8,128)(2,1)}, u32[]{:S(2)}, u32[]{:S(2)}) %all-to-all-start.4) | async-done | bytes 524320 | tf_op jit(solution)/shard_map/all_to_all | solution.py:106
  275.5 4.5 %collective-permute-start.1 = (bf16[1,1,8,8,256]{4,0,3,2,1:T(2,128)(2,1)S(1)}, bf16[1,1,8,8,256]{4,0,3,2,1:T(2,128)(2,1)S(1)}, u32[]{:S(2)}, u32[]{:S(2)}) collective-permute-start(bf16[1,1,8,8,256]{4,0,3,2,1:T(2,128)(2,1)S(1)} %get-tuple-element.97), channel_id=1, source_target_pairs={{1,0},{2,1},{3,2},{4,3},{5,4},{6,5},{7,6},{8,7},{9,8},{10,9},{11,1... | collective-permute-start | bytes 98312 | tf_op jit(solution)/shard_map/ppermute | solution.py:20
  280.0 5.6 %collective-permute-start = (bf16[1,1,8,8,256]{4,0,3,2,1:T(2,128)(2,1)S(1)}, bf16[1,1,8,8,256]{4,0,3,2,1:T(2,128)(2,1)S(1)}, u32[]{:S(2)}, u32[]{:S(2)}) collective-permute-start(bf16[1,1,8,8,256]{4,0,3,2,1:T(2,128)(2,1)S(1)} %get-tuple-element.96), channel_id=1, source_target_pairs={{0,1},{1,2},{2,3},{3,4},{4,5},{5,6},{6,7},{7,8},{8,9},{9,10},{10,1... | collective-permute-start | bytes 98312 | tf_op jit(solution)/shard_map/ppermute | solution.py:17
  286.9 3.2 %fusion.42 = bf16[1,2,8,8,256]{4,0,3,2,1:T(2,128)(2,1)S(1)} fusion(bf16[3,3,3,256,256]{4,3,2,1,0:T(8,128)(2,1)S(1)} %copy-done, bf16[1,1,8,8,256]{4,0,3,2,1:T(2,128)(2,1)S(1)} %collective-permute-done.1, bf16[1,2,8,8,256]{4,0,3,2,1:T(2,128)(2,1)S(1)} %broadcast_select_fusion, bf16[1,1,8,8,256]{4,0,3,2,1:T(2,128)(2,1)S(1)} %collective-permute-done, ...), kind=kOutput, calls=%fused_computation.40 | convolution fusion | flops 381157376 | bytes 3735554 | tf_op jit(solution)/shard_map/conv_general_dilated | solution.py:125
  (76 shorter events, 60.2 us)
Async XLA Ops:
  0.0 286.9 %copy-start = (bf16[3,3,3,256,256]{4,3,2,1,0:T(8,128)(2,1)S(1)}, bf16[3,3,3,256,256]{4,3,2,1,0:T(8,128)(2,1)}, u32[]{:S(2)}) copy-start(bf16[3,3,3,256,256]{4,3,2,1,0:T(8,128)(2,1)} %param.18) | copy-start | bytes 10616836
  2.4 41.0 %all-to-all-start = ((bf16[1,128,32,128]{1,3,0,2:T(8,128)(2,1)}), bf16[1,128,32,128]{1,3,0,2:T(8,128)(2,1)}, u32[]{:S(2)}, u32[]{:S(2)}) async-start(bf16[1,128,32,128]{1,3,0,2:T(8,128)(2,1)} %bitcast.98), calls=%async_computation | async-start | bytes 2097152 | tf_op jit(solution)/shard_map/all_to_all | solution.py:91
  43.4 34.0 %all-to-all-start.1 = ((bf16[1,128,32,128]{1,3,0,2:T(8,128)(2,1)}), bf16[1,128,32,128]{1,3,0,2:T(8,128)(2,1)}, u32[]{:S(2)}, u32[]{:S(2)}) async-start(bf16[1,128,32,128]{1,3,0,2:T(8,128)(2,1)} %bitcast.97), calls=%async_computation.1 | async-start | bytes 2097152 | tf_op jit(solution)/shard_map/all_to_all | solution.py:92
  49.3 34.0 %copy-start.6 = (s32[8]{0:T(128)S(1)}, s32[8]{0:T(128)}, u32[]{:S(2)}) copy-start(s32[8]{0:T(128)} %param.20) | copy-start | bytes 100
  49.3 36.6 %copy-start.4 = (s32[8]{0:T(128)S(1)}, s32[8]{0:T(128)}, u32[]{:S(2)}) copy-start(s32[8]{0:T(128)} %param.19) | copy-start | bytes 100
  77.5 34.0 %all-to-all-start.2 = ((bf16[1,128,32,128]{1,3,0,2:T(8,128)(2,1)}), bf16[1,128,32,128]{1,3,0,2:T(8,128)(2,1)}, u32[]{:S(2)}, u32[]{:S(2)}) async-start(bf16[1,128,32,128]{1,3,0,2:T(8,128)(2,1)} %bitcast.96), calls=%async_computation.2 | async-start | bytes 2097152 | tf_op jit(solution)/shard_map/all_to_all | solution.py:93
  117.2 2.2 copy-start.1
  125.2 2.2 copy-start.1
  133.2 2.2 copy-start.1
  141.2 2.2 copy-start.1
  149.2 2.2 copy-start.1
  157.2 2.2 copy-start.1
  165.2 2.2 copy-start.1
  173.2 2.2 copy-start.1
  207.0 8.0 %copy-start.7 = (s32[8]{0:T(128)S(1)}, s32[8]{0:T(128)}, u32[]{:S(2)}) copy-start(s32[8]{0:T(128)} %param.21) | copy-start | bytes 100
  209.2 33.9 %all-to-all-start.3 = ((bf16[32,2,8192]{2,1,0:T(2,128)(2,1)}), bf16[32,2,8192]{2,1,0:T(2,128)(2,1)}, u32[]{:S(2)}, u32[]{:S(2)}) async-start(bf16[32,2,8192]{2,1,0:T(2,128)(2,1)} %reshape.181), calls=%async_computation.3 | async-start | bytes 2097152 | tf_op jit(solution)/shard_map/all_to_all | solution.py:97
  257.9 2.9 copy-start.2
  257.9 2.9 copy-start.3
  257.9 2.9 copy-start.5
  262.2 12.1 %all-to-all-start.4 = ((bf16[8,1,128,256]{3,2,1,0:T(8,128)(2,1)}), bf16[8,1,128,256]{3,2,1,0:T(8,128)(2,1)}, u32[]{:S(2)}, u32[]{:S(2)}) async-start(bf16[8,1,128,256]{3,2,1,0:T(8,128)(2,1)} %stack.2), calls=%async_computation.4 | async-start | bytes 1048576 | tf_op jit(solution)/shard_map/all_to_all | solution.py:106
  275.5 10.1 %collective-permute-start.1 = (bf16[1,1,8,8,256]{4,0,3,2,1:T(2,128)(2,1)S(1)}, bf16[1,1,8,8,256]{4,0,3,2,1:T(2,128)(2,1)S(1)}, u32[]{:S(2)}, u32[]{:S(2)}) collective-permute-start(bf16[1,1,8,8,256]{4,0,3,2,1:T(2,128)(2,1)S(1)} %get-tuple-element.97), channel_id=1, source_target_pairs={{1,0},{2,1},{3,2},{4,3},{5,4},{6,5},{7,6},{8,7},{9,8},{10,9},{11,1... | collective-permute-start | bytes 98312 | tf_op jit(solution)/shard_map/ppermute | solution.py:20
  280.0 6.9 %collective-permute-start = (bf16[1,1,8,8,256]{4,0,3,2,1:T(2,128)(2,1)S(1)}, bf16[1,1,8,8,256]{4,0,3,2,1:T(2,128)(2,1)S(1)}, u32[]{:S(2)}, u32[]{:S(2)}) collective-permute-start(bf16[1,1,8,8,256]{4,0,3,2,1:T(2,128)(2,1)S(1)} %get-tuple-element.96), channel_id=1, source_target_pairs={{0,1},{1,2},{2,3},{3,4},{4,5},{5,6},{6,7},{7,8},{8,9},{9,10},{10,1... | collective-permute-start | bytes 98312 | tf_op jit(solution)/shard_map/ppermute | solution.py:17
